TPU v7x, 32 devices: a whole 2x2x4 slice. The times are simulated.
32 devices in a mesh: groups: 2 (over y), col: 4 (over z), row: 4 (over x, core).
Axes of the slice: x: 2, y: 2, z: 4, core: 2. Of those that a mesh axis runs over, the one named last changes fastest.
Arguments:
- diag_block: float32 [256, 256], P('row', 'col'), as said below
- panel_low: float32 [16384, 256], P(('groups', 'row'), 'col'), parts along dimension 0, may hold values from -1.5 to 1.5
- slab_rows: float32 [512, 16384], P('col', ('groups', 'row')), parts along dimension 1, may hold values from -6 to 6
- rhs_top: float32 [512, 256], P(('groups', 'col'), 'row'), parts along dimension 0, may hold values from -6 to 6
- rhs_low: float32 [256, 16384], P('col', ('groups', 'row')), parts along dimension 1, may hold values from -6 to 6
Outputs:
- panel_factor: float32 [16384, 256], P(('groups', 'row'), 'col'), parts along dimension 0
- slab_update: float32 [512, 16384], P('col', ('groups', 'row')), parts along dimension 1
- rhs_solved: float32 [512, 256], P(('groups', 'col'), 'row'), parts along dimension 0
- rhs_update: float32 [256, 16384], P('col', ('groups', 'row')), parts along dimension 1
There are 2 independent parts, one for each index of `groups`. A program takes and returns all parts, laid end to end along the dimension named above; an argument that names none is the same for every part. Nothing has to cross between parts.
Inputs may be any that keep to these rules, and one draw needn't show every extreme that they name: diag_block is symmetric and positive definite, the sum of a positive definite kernel matrix and a positive diagonal.
All inputs are finite; a program needn't handle non-finite values.
Results may differ from a plain program's by a relative error of at most 0.00015.
Values sent between devices are 32-bit elements; how exact they have to be, the bound alone decides.
A program may use at most 64 MiB of HBM per device.

v0:
```python
import jax
import jax.numpy as jnp
from jax import lax
from jax.sharding import PartitionSpec as P


def spread(x, axis, root):
    mine = lax.axis_index(axis) == root
    return lax.psum(jnp.where(mine, x, jnp.zeros_like(x)), axis)


def solve_right(factor, rows):
    return jax.scipy.linalg.solve_triangular(factor, rows.T, lower=True).T


def times_transpose(left_rows, lower_panel):
    return jnp.dot(
        left_rows,
        lower_panel.T,
        precision=lax.Precision.HIGHEST,
        preferred_element_type=jnp.float32,
    )


def local(diag_block, panel_low, slab_rows, rhs_top, rhs_low):
    diag_tiles = lax.all_gather(diag_block, "col", axis=1, tiled=True)
    whole_block = lax.all_gather(diag_tiles, "row", axis=0, tiled=True)
    factor = jnp.linalg.cholesky(whole_block)
    regrouped = lax.all_to_all(panel_low, "col", split_axis=0, concat_axis=1, tiled=True)
    solved_part = solve_right(factor, regrouped)
    lower_panel = lax.all_gather(solved_part, "col", axis=0, tiled=True)
    panel_width = panel_low.shape[1]
    col_index = lax.axis_index("col")
    panel_factor = lax.dynamic_slice_in_dim(lower_panel, col_index * panel_width, panel_width, 1)
    slab_count = slab_rows.shape[0]
    rows_here = lower_panel.shape[0]
    first_row = col_index * slab_count
    root_row = first_row // rows_here
    offset = first_row - root_row * rows_here
    my_rows = lax.dynamic_slice_in_dim(lower_panel, offset, slab_count, 0)
    slab_left = spread(my_rows, "row", root_row)
    top_rhs = lax.all_gather(rhs_top, "row", axis=1, tiled=True)
    solved_top = solve_right(factor, top_rhs)
    top_width = rhs_top.shape[1]
    rhs_solved = lax.dynamic_slice_in_dim(
        solved_top, lax.axis_index("row") * top_width, top_width, 1
    )
    slab_update = slab_rows - times_transpose(slab_left, lower_panel)
    rhs_update = rhs_low - times_transpose(solved_top, lower_panel)
    return (panel_factor, slab_update, rhs_solved, rhs_update)


def solution(mesh):
    placed = (
        P("row", "col"),
        P(("groups", "row"), "col"),
        P("col", ("groups", "row")),
        P(("groups", "col"), "row"),
        P("col", ("groups", "row")),
    )
    return jax.shard_map(
        local,
        mesh=mesh,
        in_specs=placed,
        out_specs=(
            P(("groups", "row"), "col"),
            P("col", ("groups", "row")),
            P(("groups", "col"), "row"),
            P("col", ("groups", "row")),
        ),
        check_vma=False,
    )
```

profile of v0, /device:TPU:0, one launch (start us, length us, event | category | flops | bytes accessed | tf_op | source)
XLA Modules:
  0.0 193.8 jit_solution(9213164207617818367)
XLA Ops:
  7.2 1.9 copy.28
  9.1 6.3 %all-to-all-start = ((f32[4,512,64]{1,2,0:T(8,128)}), f32[4,512,64]{1,2,0:T(8,128)S(1)}, u32[]{:S(2)}, u32[]{:S(2)}) async-start(f32[4,512,64]{1,2,0:T(8,128)} %bitcast.45), calls=%async_computation | async-start | bytes 1048576 | tf_op jit(solution)/shard_map/all_to_all | solution.py:29
  15.5 20.8 %all_gather.12 = f32[64,256]{0,1:T(8,128)S(1)} all-gather(f32[64,64]{0,1:T(8,128)S(1)} %copy.20), channel_id=1, replica_groups=mesh['groups'=2,'col'=4,'row'=4] {'col'}, dimensions={1}, use_global_device_ids=true | all-gather | bytes 81920 | tf_op jit(solution)/shard_map/all_gather | solution.py:26
  36.4 5.8 %all_gather.13 = f32[256,256]{1,0:T(8,128)S(1)} all-gather(f32[64,256]{1,0:T(8,128)S(1)} %copy.21), channel_id=1, replica_groups=mesh['groups'=2,'col'=4,'row'=4] {'row'}, dimensions={0}, use_global_device_ids=true | all-gather | bytes 327680 | tf_op jit(solution)/shard_map/all_gather | solution.py:27
  42.4 11.7 %cholesky.50 = f32[128,128]{1,0:T(8,128)S(1)} custom-call(f32[128,128]{1,0:T(8,128)S(1)} %cholesky.118), custom_call_target="Cholesky" | custom-call | tf_op jit(solution)/shard_map/jit(cholesky)/cholesky | solution.py:28
  54.1 9.8 %custom-call.18 = f32[1,128,128]{1,2,0:T(8,128)S(1)} custom-call(f32[1,128,128]{2,1,0:T(8,128)S(1)} %get-tuple-element.25), custom_call_target="InvertDiagBlocksLowerTriangular" | custom-call | tf_op jit(solution)/shard_map/jit(cholesky)/cholesky | solution.py:28
  64.4 11.7 %cholesky.105 = f32[128,128]{1,0:T(8,128)S(1)} custom-call(f32[128,128]{1,0:T(8,128)S(1)} %convolution_subtract_fusion.3), custom_call_target="Cholesky" | custom-call | tf_op jit(solution)/shard_map/jit(cholesky)/cholesky | solution.py:28
  76.2 0.6 compare_reduce_fusion
  78.2 4.1 %while.1 = (s32[]{:T(128)}, f32[256,256]{1,0:T(8,128)S(1)}, s32[2,2]{1,0:T(2,128)S(1)}, f32[2,128,128]{2,1,0:T(8,128)S(1)}, s32[]{:T(128)}) while((s32[]{:T(128)}, f32[256,256]{1,0:T(8,128)S(1)}, s32[2,2]{1,0:T(2,128)S(1)}, f32[2,128,128]{2,1,0:T(8,128)S(1)}, s32[]{:T(128)}) %tuple.27), condition=%wide.while_cond, body=%wide.while_body.sunk | while | flops 2 | bytes 131181 | solution.py:13
  78.4 0.6 fusion.26
  79.0 1.4 bitcast_dynamic-update-slice_fusion.2
  80.4 0.6 fusion.26
  81.0 1.4 bitcast_dynamic-update-slice_fusion.2
  82.4 19.7 %custom-call.19 = f32[2,128,128]{1,2,0:T(8,128)S(1)} custom-call(f32[2,128,128]{2,1,0:T(8,128)S(1)} %get-tuple-element.11), custom_call_target="InvertDiagBlocksLowerTriangular" | custom-call | tf_op jit(solution)/shard_map/jit(_solve_triangular)/triangular_solve | solution.py:13
  102.9 0.4 fusion.8
  103.3 0.8 maximum_bitcast_fusion
  104.3 5.4 %all_gather.15 = f32[64,256]{0,1:T(8,128)S(1)} all-gather(f32[64,64]{0,1:T(8,128)S(1)} %copy.24), channel_id=1, replica_groups=mesh['groups'=2,'col'=4,'row'=4] {'row'}, dimensions={1}, use_global_device_ids=true | all-gather | bytes 81920 | tf_op jit(solution)/shard_map/all_gather | solution.py:42
  110.5 0.7 fusion.12
  111.2 39.3 %all-gather.2.cloned.1.call-done = f32[2048,256]{0,1:T(8,128)} async-done(((f32[512,256]{0,1:T(8,128)}), f32[2048,256]{0,1:T(8,128)}) %all-gather.2.cloned.1.call-update) | async-done | bytes 2097168 | tf_op jit(solution)/shard_map/all_gather | solution.py:31
  150.5 1.7 dynamic-slice_select_fusion
  152.3 3.9 %convolution_subtract_fusion.1 = f32[64,2048]{1,0:T(8,128)} fusion(f32[64,2048]{1,0:T(8,128)} %param.9, f32[2048,256]{0,1:T(8,128)} %all-gather.2.cloned.1.call-done, f32[128,64]{0,1:T(8,128)S(1)} %fusion.7, f32[128,64]{0,1:T(8,128)S(1)} %fusion.6), kind=kOutput, calls=%fused_computation.3 | convolution fusion | flops 402800640 | bytes 3211264 | tf_op jit(solution)/shard_map/dot_general | solution.py:17
  156.2 0.8 constant_dynamic-slice_fusion.1
  157.0 26.8 %all-reduce.3.cloned.1.call-done = f32[128,256]{0,1:T(8,128)} async-done(((f32[128,256]{0,1:T(8,128)}), f32[128,256]{0,1:T(8,128)}) %all-reduce.3.cloned.1.call-update) | async-done | bytes 131088 | tf_op jit(solution)/shard_map/psum | solution.py:9
  183.8 3.1 %convolution_subtract_fusion = f32[128,2048]{1,0:T(8,128)} fusion(f32[128,2048]{1,0:T(8,128)S(1)} %copy-done.1, f32[128,256]{0,1:T(8,128)} %all-reduce.3.cloned.1.call-done, f32[2048,256]{0,1:T(8,128)S(1)} %copy-done), kind=kOutput, calls=%fused_computation.2 | convolution fusion | flops 805568512 | bytes 4325376 | tf_op jit(solution)/shard_map/dot_general | solution.py:17
  (36 shorter events, 2.7 us)
Async XLA Ops:
  7.2 8.2 %copy-start.2 = (f32[64,64]{1,0:T(8,128)S(1)}, f32[64,64]{1,0:T(8,128)}, u32[]{:S(2)}) copy-start(f32[64,64]{1,0:T(8,128)} %param.5) | copy-start | bytes 49156
  9.1 93.0 %all-to-all-start = ((f32[4,512,64]{1,2,0:T(8,128)}), f32[4,512,64]{1,2,0:T(8,128)S(1)}, u32[]{:S(2)}, u32[]{:S(2)}) async-start(f32[4,512,64]{1,2,0:T(8,128)} %bitcast.45), calls=%async_computation | async-start | bytes 1048576 | tf_op jit(solution)/shard_map/all_to_all | solution.py:29
  15.4 135.1 %all-gather.2.cloned.1.call-start = ((), (), s32[]{:S(2)}) async-start(), calls=%async_computation.1 | async-start | bytes 2621440 | tf_op jit(solution)/shard_map/all_gather | solution.py:31
  78.2 26.0 %copy-start.3 = (f32[64,64]{1,0:T(8,128)S(1)}, f32[64,64]{1,0:T(8,128)}, u32[]{:S(2)}) copy-start(f32[64,64]{1,0:T(8,128)} %param.8) | copy-start | bytes 49156
  104.2 79.6 %all-reduce.3.cloned.1.call-start = ((), (), s32[]{:S(2)}) async-start(), calls=%async_computation.2 | async-start | bytes 262144 | tf_op jit(solution)/shard_map/psum | solution.py:9
  150.5 5.7 %copy-start = (f32[2048,256]{0,1:T(8,128)S(1)}, f32[2048,256]{0,1:T(8,128)}, u32[]{:S(2)}) copy-start(f32[2048,256]{0,1:T(8,128)} %all-gather.2.cloned.1.call-done) | copy-start | bytes 6291460
  152.3 31.6 %copy-start.1 = (f32[128,2048]{1,0:T(8,128)S(1)}, f32[128,2048]{1,0:T(8,128)}, u32[]{:S(2)}) copy-start(f32[128,2048]{1,0:T(8,128)} %param.7) | copy-start | bytes 3145732
Sparse Core Ops, SparseCore 0:
  104.3 46.1 all-gather.1
  153.4 30.3 all-reduce.2
where the time goes:
time: 194 us
  waiting for transfers between devices  66.1 us (34%)
  other arithmetic  57 us (29%)
  blocking collectives  32 us (16%)
  between operations  15.5 us (8%)
  matrix products  9.34 us (5%)
  local copies, waits for them, and re-layouts  7.21 us (4%)
  starting transfers between devices  6.36 us (3%)
    all_gather x1, waiting for transfers between devices, local(): lower_panel = lax.all_gather(solved_part, 'col', axis=0, tiled=True)  39.3 us
    another operation x6, other arithmetic, local(): factor = jnp.linalg.cholesky(whole_block)  34 us
    psum x1, waiting for transfers between devices, spread(): return lax.psum(jnp.where(mine, x, jnp.zeros_like(x)), axis)  26.8 us
    all_gather x1, blocking collectives, local(): diag_tiles = lax.all_gather(diag_block, 'col', axis=1, tiled=True)  20.8 us
    another operation x3, other arithmetic, solve_right(): return jax.scipy.linalg.solve_triangular(factor, rows.T, lower=True).T  19.7 us
    dot_general x2, matrix products, times_transpose(): jnp.dot(left_rows, lower_panel.T, precision=lax.Precision.HIGHEST, prefer...  7.05 us
    all_to_all x1, starting transfers between devices, local(): lax.all_to_all(panel_low, 'col', split_axis=0, concat_axis=1, tiled=True)  6.32 us
    all_gather x1, blocking collectives, local(): whole_block = lax.all_gather(diag_tiles, 'row', axis=0, tiled=True)  5.79 us
  transfers between devices with their start and end apart: 3, of which 2 were waited for; matrix products, arithmetic and copies ran while one was open for 33% of the time, Pallas kernels for 0%

commit v1 on v0

v1 whole, which is shorter than its diff:
```python
import functools

import jax
import jax.numpy as jnp
from jax import lax
from jax.experimental import pallas as pl
from jax.experimental.pallas import tpu as pltpu
from jax.sharding import PartitionSpec as P

MESH = pl.DeviceIdType.MESH
BS = 64
CHUNKS = 4
HIGH = lax.Precision.HIGHEST


def dot(a, b, contract=((1,), (0,))):
    return lax.dot_general(
        a, b, (contract, ((), ())), precision=HIGH, preferred_element_type=jnp.float32
    )


def eliminate(block, between):
    row = lax.broadcasted_iota(jnp.int32, (BS, 2 * BS), 0)
    lane = lax.broadcasted_iota(jnp.int32, (BS, 2 * BS), 1)
    eye = jnp.where(row[:, :BS] == lane[:, :BS], 1.0, 0.0).astype(jnp.float32)
    y = jnp.concatenate([block, eye], axis=1)
    groups = [y[g * 8 : g * 8 + 8] for g in range(BS // 8)]
    sub = row[:8]
    for k in range(BS):
        if k % 16 == 0:
            between(k // 16)
        g0, s0 = k // 8, k % 8
        pivot_row = groups[g0][s0 : s0 + 1, :]
        d = pivot_row[:, k : k + 1]
        scale = lax.rsqrt(d)
        r = pivot_row * scale
        col = groups[g0][:, k : k + 1] * scale
        groups[g0] = jnp.where(
            sub == s0,
            jnp.broadcast_to(r, (8, 2 * BS)),
            groups[g0] - jnp.where(sub > s0, col, 0.0) * r,
        )
        for g in range(g0 + 1, BS // 8):
            groups[g] = groups[g] - (groups[g][:, k : k + 1] * scale) * r
    return jnp.concatenate(groups, axis=0)[:, BS:]


def gather_kernel(
    ncol, nrow, pack, slab_count,
    diag_ref, panel_ref, rhs_ref,
    pt_ref, lr_ref, rs_ref,
    dpack, dslots, raw, left, rslots, aug, linv,
    dsend, drecv, rsend, rrecv, l1send, l1recv, l2send, l2recv, usend, wsend, precv,
):
    mc = lax.axis_index("col")
    mr = lax.axis_index("row")
    n = ncol * nrow
    me = mc * nrow + mr
    dr, dc = diag_ref.shape
    rows, w = panel_ref.shape
    nb = w * ncol
    chunk = rows // CHUNKS
    rk = rhs_ref.shape[1]

    def peer(t):
        p = lax.rem(me + t, n)
        return p // nrow, lax.rem(p, nrow), p

    barrier = pltpu.get_barrier_semaphore()

    def greet(t, carry):
        pc, pr, _ = peer(t)
        pl.semaphore_signal(barrier, inc=1, device_id={"col": pc, "row": pr}, device_id_type=MESH)
        return carry

    lax.fori_loop(1, n, greet, 0)

    x = diag_ref[...]
    step = dr // pack
    dpack[...] = jnp.concatenate([x[i * step : (i + 1) * step] for i in range(pack)], axis=1)
    dslots[me] = dpack[...]
    rslots[mr] = rhs_ref[...]
    mine = pl.ds(pl.multiple_of(mc * w, w), w)
    raw[mine, :] = panel_ref[...].T
    root = (mc * slab_count) // rows

    pl.semaphore_wait(barrier, n - 1)

    def diag_copy(t):
        pc, pr, p = peer(t)
        return pltpu.make_async_remote_copy(
            dpack, dslots.at[me], dsend.at[t], drecv.at[me],
            device_id={"col": pc, "row": pr}, device_id_type=MESH,
        )

    def diag_wait(p):
        return pltpu.make_async_remote_copy(
            dpack, dslots.at[p], dsend.at[0], drecv.at[p],
            device_id={"col": mc, "row": mr}, device_id_type=MESH,
        )

    def rhs_copy(t, slot):
        return pltpu.make_async_remote_copy(
            rhs_ref, rslots.at[slot], rsend.at[t], rrecv.at[slot],
            device_id={"col": mc, "row": lax.rem(mr + t, nrow)}, device_id_type=MESH,
        )

    def left_piece(t, k):
        c = lax.rem(mc + t, ncol)
        off = pl.multiple_of(lax.rem(c * slab_count, rows), slab_count)
        at = pl.ds(pl.multiple_of(k * w, w), w)
        return pltpu.make_async_remote_copy(
            raw.at[mine, pl.ds(off, slab_count)], left.at[at, :],
            l1send.at[t], l1recv.at[k],
            device_id={"col": c, "row": mr}, device_id_type=MESH,
        )

    def left_whole(t):
        return pltpu.make_async_remote_copy(
            left, left, l2send.at[t], l2recv,
            device_id={"col": mc, "row": lax.rem(mr + t, nrow)}, device_id_type=MESH,
        )

    def piece(block, q, sends, to):
        part = raw.at[
            pl.ds(pl.multiple_of(block * w, w), w),
            pl.ds(pl.multiple_of(q * chunk, chunk), chunk),
        ]
        return pltpu.make_async_remote_copy(
            part, part, sends.at[block, q], precv.at[block, q],
            device_id={"col": to, "row": mr}, device_id_type=MESH,
        )

    def loop(lo, hi, body):
        def run(i, carry):
            body(i)
            return carry

        lax.fori_loop(lo, hi, run, 0)

    loop(1, n, lambda t: diag_copy(t).start())

    def left_root(t):
        return ((lax.rem(mc + t, ncol)) * slab_count) // rows == mr

    def send_left(t):
        @pl.when(left_root(t))
        def _():
            left_piece(t, mc).start()

    loop(1, ncol, send_left)

    @pl.when(root == mr)
    def _():
        off = pl.multiple_of(lax.rem(mc * slab_count, rows), slab_count)
        left[mine, :] = raw[mine, pl.ds(off, slab_count)]

    loop(1, nrow, lambda t: rhs_copy(t, mr).start())

    def send_own(q):
        @pl.when(mc + 1 < ncol)
        def _():
            piece(mc, q, usend, mc + 1).start()

        @pl.when(mc > 0)
        def _():
            piece(mc, q, wsend, mc - 1).start()

    loop(0, CHUNKS, send_own)

    events = (ncol - 1) * CHUNKS
    points = (nb // BS) * (BS // 16)
    each = -(-events // points)

    def forward(e):
        s = e // CHUNKS + 1
        q = lax.rem(e, CHUNKS)

        @pl.when(jnp.logical_and(mc - s >= 0, mc + 1 < ncol))
        def _():
            piece(mc - s, q, usend, mc + 1).wait_recv()
            piece(mc - s, q, usend, mc + 1).start()

        @pl.when(jnp.logical_and(mc + s < ncol, mc > 0))
        def _():
            piece(mc + s, q, wsend, mc - 1).wait_recv()
            piece(mc + s, q, wsend, mc - 1).start()

    loop(1, n, lambda t: diag_wait(peer(t)[2]).wait_recv())

    for r in range(nrow):
        parts = []
        for c in range(ncol):
            v = dslots[c * nrow + r]
            parts.append(
                jnp.concatenate([v[:, i * dc : (i + 1) * dc] for i in range(pack)], axis=0)
            )
        aug[r * dr : (r + 1) * dr, :nb] = jnp.concatenate(parts, axis=1)
    ri = lax.broadcasted_iota(jnp.int32, (nb, nb), 0)
    ci = lax.broadcasted_iota(jnp.int32, (nb, nb), 1)
    aug[:, nb:] = jnp.where(ri == ci, 1.0, 0.0).astype(jnp.float32)

    def block_step(b):
        @pl.when(jnp.logical_and(b == 1, root == mr))
        def _():
            def wait_piece(t):
                left_piece(t, lax.rem(mc + t, ncol)).wait_recv()

            loop(1, ncol, wait_piece)
            loop(1, nrow, lambda t: left_whole(t).start())

        here = pl.ds(pl.multiple_of(b * BS, BS), BS)
        panel = aug[here, :]
        rolled = pltpu.roll(panel[:, :nb], lax.rem(nb - b * BS, nb), 1)

        def between(i):
            point = b * (BS // 16) + i
            loop(
                jnp.minimum(point * each, events),
                jnp.minimum((point + 1) * each, events),
                forward,
            )

        winv = eliminate(rolled[:, :BS], between)
        upper = dot(winv, panel)
        linv[here, :] = upper[:, nb:]
        lane = lax.broadcasted_iota(jnp.int32, (BS, nb), 1)
        later = jnp.where(lane >= (b + 1) * BS, upper[:, :nb], 0.0)
        aug[...] = aug[...] - dot(later, upper, ((0,), (0,)))

    loop(0, nb // BS, block_step)

    @pl.when(root != mr)
    def _():
        left_whole(0).wait_recv()

    loop(1, nrow, lambda t: rhs_copy(t, lax.rem(mr + t, nrow)).wait_recv())
    inv = linv[...]
    top = jnp.concatenate([rslots[r].T for r in range(nrow)], axis=0)
    left_t = dot(inv, left[...])
    top_t = dot(inv, top)
    lr_ref[:slab_count, :] = left_t.T
    rt = top_t.T
    lr_ref[slab_count:, :] = rt
    picked = pltpu.roll(rt, lax.rem(nb - mr * rk, nb), 1)
    rs_ref[...] = picked[:, :rk]

    def finish(q):
        def arrived(t):
            block = lax.rem(mc + t, ncol)

            @pl.when(jnp.logical_or(
                jnp.logical_and(block < mc, mc + 1 >= ncol),
                jnp.logical_and(block > mc, mc <= 0),
            ))
            def _():
                piece(block, q, usend, mc).wait_recv()

        loop(1, ncol, arrived)
        at = pl.ds(pl.multiple_of(q * chunk, chunk), chunk)
        pt_ref[:, at] = dot(linv[...], raw[:, at])

    loop(0, CHUNKS, finish)

    loop(1, n, lambda t: diag_copy(t).wait_send())
    loop(1, nrow, lambda t: rhs_copy(t, mr).wait_send())

    def sent_left(t):
        @pl.when(left_root(t))
        def _():
            left_piece(t, mc).wait_send()

    loop(1, ncol, sent_left)

    @pl.when(root == mr)
    def _():
        loop(1, nrow, lambda t: left_whole(t).wait_send())

    def sent(block):
        def chunk_sent(q):
            @pl.when(jnp.logical_and(block <= mc, mc + 1 < ncol))
            def _():
                piece(block, q, usend, mc + 1).wait_send()

            @pl.when(jnp.logical_and(block >= mc, mc > 0))
            def _():
                piece(block, q, wsend, mc - 1).wait_send()

        loop(0, CHUNKS, chunk_sent)

    loop(0, ncol, sent)


def update_kernel(w, slab_count, pt_ref, lr_ref, rs_ref, slab_ref, low_ref,
                  pf_ref, su_ref, rso_ref, ru_ref):
    mc = lax.axis_index("col")
    prod = dot(lr_ref[...], pt_ref[...])
    su_ref[...] = slab_ref[...] - prod[:slab_count]
    ru_ref[...] = low_ref[...] - prod[slab_count:]
    pf_ref[...] = pt_ref[pl.ds(pl.multiple_of(mc * w, w), w), :].T
    rso_ref[...] = rs_ref[...]


def local(ncol, nrow, diag_block, panel_low, slab_rows, rhs_top, rhs_low):
    dr, dc = diag_block.shape
    rows, w = panel_low.shape
    nb = w * ncol
    slab_count = slab_rows.shape[0]
    nrhs, rk = rhs_top.shape
    pack = 128 // dc
    if dr % (8 * pack):
        pack = 1
    n = ncol * nrow
    f32 = jnp.float32
    vm = pl.BlockSpec(memory_space=pltpu.VMEM)
    dma = pltpu.SemaphoreType.DMA
    pt, lr, rs = pl.pallas_call(
        functools.partial(gather_kernel, ncol, nrow, pack, slab_count),
        out_shape=(
            jax.ShapeDtypeStruct((nb, rows), f32),
            jax.ShapeDtypeStruct((slab_count + nrhs, nb), f32),
            jax.ShapeDtypeStruct((nrhs, rk), f32),
        ),
        in_specs=[vm] * 3,
        out_specs=(vm,) * 3,
        scratch_shapes=[
            pltpu.VMEM((dr // pack, dc * pack), f32),
            pltpu.VMEM((n, dr // pack, dc * pack), f32),
            pltpu.VMEM((nb, rows), f32),
            pltpu.VMEM((nb, slab_count), f32),
            pltpu.VMEM((nrow, nrhs, rk), f32),
            pltpu.VMEM((nb, 2 * nb), f32),
            pltpu.VMEM((nb, nb), f32),
            dma((n,)), dma((n,)),
            dma((nrow,)), dma((nrow,)),
            dma((ncol,)), dma((ncol,)),
            dma((nrow,)), dma,
            dma((ncol, CHUNKS)), dma((ncol, CHUNKS)), dma((ncol, CHUNKS)),
        ],
        compiler_params=pltpu.CompilerParams(
            collective_id=0, has_side_effects=True, vmem_limit_bytes=40 * 1024 * 1024
        ),
    )(diag_block, panel_low, rhs_top)
    tile = rows // 4
    return pl.pallas_call(
        functools.partial(update_kernel, w, slab_count),
        grid=(4,),
        out_shape=(
            jax.ShapeDtypeStruct((rows, w), f32),
            jax.ShapeDtypeStruct(slab_rows.shape, f32),
            jax.ShapeDtypeStruct((nrhs, rk), f32),
            jax.ShapeDtypeStruct(rhs_low.shape, f32),
        ),
        in_specs=[
            pl.BlockSpec((nb, tile), lambda i: (0, i)),
            pl.BlockSpec((slab_count + nrhs, nb), lambda i: (0, 0)),
            pl.BlockSpec((nrhs, rk), lambda i: (0, 0)),
            pl.BlockSpec((slab_count, tile), lambda i: (0, i)),
            pl.BlockSpec((nrhs, tile), lambda i: (0, i)),
        ],
        out_specs=(
            pl.BlockSpec((tile, w), lambda i: (i, 0)),
            pl.BlockSpec((slab_count, tile), lambda i: (0, i)),
            pl.BlockSpec((nrhs, rk), lambda i: (0, 0)),
            pl.BlockSpec((nrhs, tile), lambda i: (0, i)),
        ),
        compiler_params=pltpu.CompilerParams(vmem_limit_bytes=32 * 1024 * 1024),
    )(pt, lr, rs, slab_rows, rhs_low)


def solution(mesh):
    ncol, nrow = mesh.shape["col"], mesh.shape["row"]
    return jax.shard_map(
        functools.partial(local, ncol, nrow),
        mesh=mesh,
        in_specs=(
            P("row", "col"),
            P(("groups", "row"), "col"),
            P("col", ("groups", "row")),
            P(("groups", "col"), "row"),
            P("col", ("groups", "row")),
        ),
        out_specs=(
            P(("groups", "row"), "col"),
            P("col", ("groups", "row")),
            P(("groups", "col"), "row"),
            P("col", ("groups", "row")),
        ),
        check_vma=False,
    )
```

time: 194 us -> 62.2 us (0.32)
  the two profiles are of different devices: /device:TPU:0 before, /device:TPU:8 now
where the time goes in v1:
time: 62.2 us; the launch traced here: 61.9 us
  Pallas kernels  57.1 us (92%)
  local copies, waits for them, and re-layouts  4.12 us (7%)
  between operations  0.69 us (1%)
    pallas_call x1, Pallas kernels, local(): pl.pallas_call(functools.partial(gather_kernel, ncol, nrow, pack, slab_co...  53.9 us
    pallas_call x1, Pallas kernels, local(): pl.pallas_call(functools.partial(update_kernel, w, slab_count), grid=(4,)...  3.25 us
    unnamed x9, local copies, waits for them, and re-layouts  3.01 us

profile of v1, /device:TPU:8, one launch (start us, length us, event | category | flops | bytes accessed | tf_op | source)
XLA Modules:
  0.0 61.9 jit_solution(15120028220286191559)
XLA Ops:
  0.6 0.0 copy-start.1
  0.6 0.0 copy-start
  0.7 1.5 %copy.9.panel_ref = f32[2048,64]{1,0:T(8,128)S(1)} copy(f32[2048,64]{0,1:T(8,128)} %param.6) | data formatting | bytes 1048576 | tf_op args[1]
  2.1 0.0 copy-start.2
  2.2 0.8 %copy-done.2 = f32[64,64]{1,0:T(8,128)S(1)} copy-done((f32[64,64]{1,0:T(8,128)S(1)}, f32[64,64]{1,0:T(8,128)}, u32[]{:S(2)}) %copy-start.2) | copy-done | bytes 16408
  2.9 0.0 copy-start.3
  2.9 0.8 %copy-done.3 = f32[64,64]{1,0:T(8,128)S(1)} copy-done((f32[64,64]{1,0:T(8,128)S(1)}, f32[64,64]{1,0:T(8,128)}, u32[]{:S(2)}) %copy-start.3) | copy-done | bytes 16408
  3.7 53.9 %shard_map.84 = (f32[256,2048]{1,0:T(8,128)S(1)}, f32[192,256]{1,0:T(8,128)S(1)}, f32[64,64]{1,0:T(8,128)S(1)}) custom-call(f32[64,64]{1,0:T(8,128)S(1)} %copy-done.2, f32[2048,64]{1,0:T(8,128)S(1)} %copy.9.panel_ref, f32[64,64]{1,0:T(8,128)S(1)} %copy-done.3), custom_call_target="tpu_custom_call" | custom-call | tf_op jit(solution)/shard_map/pallas_call | solution.py:317
  57.6 0.0 copy-done.1
  57.6 0.0 copy-done
  57.6 3.3 %shard_map.85 = (f32[2048,64]{1,0:T(8,128)S(1)}, f32[128,2048]{1,0:T(8,128)}, f32[64,64]{1,0:T(8,128)}, f32[64,2048]{1,0:T(8,128)}) custom-call(f32[256,2048]{1,0:T(8,128)S(1)} %get-tuple-element.7.pt_ref, f32[192,256]{1,0:T(8,128)S(1)} %get-tuple-element.8.lr_ref, f32[64,64]{1,0:T(8,128)S(1)} %get-tuple-element.9.rs_ref, f32[128,2048]{1,0:T(8,128)S(1)} %copy-done, ...), custom_call_target="tpu_custom_call" | custom-call | tf_op jit(solution)/shard_map/pallas_call | solution.py:345
  60.8 1.1 %copy.10 = f32[2048,64]{0,1:T(8,128)} copy(f32[2048,64]{1,0:T(8,128)S(1)} %get-tuple-element.10) | data formatting | bytes 1048576 | tf_op jit(solution)/shard_map/pallas_call | solution.py:345
Async XLA Ops:
  0.6 56.9 %copy-start.1 = (f32[64,2048]{1,0:T(8,128)S(1)}, f32[64,2048]{1,0:T(8,128)}, u32[]{:S(2)}) copy-start(f32[64,2048]{1,0:T(8,128)} %low_ref.1) | copy-start | bytes 1572868
  0.6 56.9 %copy-start = (f32[128,2048]{1,0:T(8,128)S(1)}, f32[128,2048]{1,0:T(8,128)}, u32[]{:S(2)}) copy-start(f32[128,2048]{1,0:T(8,128)} %slab_ref.1) | copy-start | bytes 3145732
  2.1 0.8 %copy-start.2 = (f32[64,64]{1,0:T(8,128)S(1)}, f32[64,64]{1,0:T(8,128)}, u32[]{:S(2)}) copy-start(f32[64,64]{1,0:T(8,128)} %diag_ref.1) | copy-start | bytes 49156
  2.9 0.8 %copy-start.3 = (f32[64,64]{1,0:T(8,128)S(1)}, f32[64,64]{1,0:T(8,128)}, u32[]{:S(2)}) copy-start(f32[64,64]{1,0:T(8,128)} %rhs_ref.1) | copy-start | bytes 49156

commit v2 on v1

v2 whole, which is shorter than its diff:
```python
import functools

import jax
import jax.numpy as jnp
from jax import lax
from jax.experimental import pallas as pl
from jax.experimental.pallas import tpu as pltpu
from jax.sharding import PartitionSpec as P

MESH = pl.DeviceIdType.MESH
BS = 64
CHUNKS = 4
PIVOTS = 8
HIGH = lax.Precision.HIGHEST


def dot(a, b, contract=((1,), (0,))):
    return lax.dot_general(
        a, b, (contract, ((), ())), precision=HIGH, preferred_element_type=jnp.float32
    )


def eliminate(block):
    shape = (8, 2 * BS)
    row = lax.broadcasted_iota(jnp.int32, (BS, BS), 0)
    lane = lax.broadcasted_iota(jnp.int32, (BS, BS), 1)
    eye = jnp.where(row == lane, 1.0, 0.0).astype(jnp.float32)
    y = jnp.concatenate([block, eye], axis=1)
    groups = [y[g * 8 : g * 8 + 8] for g in range(BS // 8)]
    sub = lax.broadcasted_iota(jnp.int32, shape, 0)

    def wide(v):
        return jnp.broadcast_to(v, shape)

    for k in range(0, BS, PIVOTS):
        g0, s0 = k // 8, k % 8
        cols = [
            {g: wide(groups[g][:, k + j : k + j + 1]) for g in range(g0, BS // 8)}
            for j in range(PIVOTS)
        ]
        rows = [wide(groups[g0][s0 + j : s0 + j + 1, :]) for j in range(PIVOTS)]
        d = [
            [wide(cols[j][g0][s0 + i : s0 + i + 1, :]) for j in range(i + 1)]
            for i in range(PIVOTS)
        ]
        for j in range(PIVOTS):
            scale = lax.rsqrt(d[j][j])
            for i in range(j + 1, PIVOTS):
                d[i][j] = d[i][j] * scale
            for i in range(j + 1, PIVOTS):
                for m in range(j + 1, i + 1):
                    d[i][m] = d[i][m] - d[i][j] * d[m][j]
            rows[j] = rows[j] * scale
            for i in range(j + 1, PIVOTS):
                rows[i] = rows[i] - d[i][j] * rows[j]
            for g in cols[j]:
                cols[j][g] = cols[j][g] * scale
                for i in range(j + 1, PIVOTS):
                    cols[i][g] = cols[i][g] - cols[j][g] * d[i][j]
        for g in range(g0, BS // 8):
            if g == g0 and s0 + PIVOTS == 8:
                new = groups[g]
            else:
                new = groups[g]
                for j in range(PIVOTS):
                    new = new - cols[j][g] * rows[j]
            if g == g0:
                new = jnp.where(sub < s0, groups[g], new)
                for j in range(PIVOTS):
                    new = jnp.where(sub == s0 + j, rows[j], new)
            groups[g] = new
    return jnp.concatenate(groups, axis=0)[:, BS:]


def gather_kernel(
    ncol, nrow, pack, slab_count,
    diag_ref, panel_ref, rhs_ref,
    pt_ref, lr_ref, rs_ref,
    dmine, dslots, raw, left, rslots, aug, linv,
    local_sem, d1send, d1recv, d2send, d2recv, rsend, rrecv,
    lsend, lrecv, usend, wsend, precv,
):
    mc = lax.axis_index("col")
    mr = lax.axis_index("row")
    dr, dc = diag_ref.shape
    w, rows = panel_ref.shape
    nb = w * ncol
    chunk = rows // CHUNKS
    rk = rhs_ref.shape[1]

    def loop(lo, hi, body):
        def run(i, carry):
            body(i)
            return carry

        lax.fori_loop(lo, hi, run, 0)

    def on_col(t):
        return {"col": lax.rem(mc + t, ncol), "row": mr}

    def on_row(t):
        return {"col": mc, "row": lax.rem(mr + t, nrow)}

    def remote(src, dst, send, recv, to):
        return pltpu.make_async_remote_copy(
            src, dst, send, recv, device_id=to, device_id_type=MESH
        )

    barrier = pltpu.get_barrier_semaphore()
    loop(1, ncol, lambda t: pl.semaphore_signal(
        barrier, inc=1, device_id=on_col(t), device_id_type=MESH))
    loop(1, nrow, lambda t: pl.semaphore_signal(
        barrier, inc=1, device_id=on_row(t), device_id_type=MESH))

    mine = pl.ds(pl.multiple_of(mc * w, w), w)
    loads = (
        pltpu.make_async_copy(diag_ref, dmine, local_sem.at[0]),
        pltpu.make_async_copy(panel_ref, raw.at[mine, :], local_sem.at[1]),
        pltpu.make_async_copy(rhs_ref, rslots.at[mr], local_sem.at[2]),
    )
    for load in loads:
        load.start()
    loads[0].wait()
    x = dmine[...]
    step = dr // pack
    dslots[mr, mc] = jnp.concatenate([x[i * step : (i + 1) * step] for i in range(pack)], axis=1)
    loads[1].wait()
    loads[2].wait()
    slab_first = mc * slab_count
    root = slab_first // rows
    slab_off = pl.multiple_of(lax.rem(slab_first, rows), slab_count)

    pl.semaphore_wait(barrier, ncol + nrow - 2)

    def diag_col(t, slot):
        at = dslots.at[mr, slot]
        return remote(at, at, d1send.at[t], d1recv.at[slot], on_col(t))

    def diag_row(t, slot):
        at = dslots.at[slot]
        return remote(at, at, d2send.at[t], d2recv.at[slot], on_row(t))

    def rhs_copy(t, slot):
        at = rslots.at[slot]
        return remote(at, at, rsend.at[t], rrecv.at[slot], on_row(t))

    def left_copy(t):
        return remote(left, left, lsend.at[t], lrecv, on_row(t))

    def piece(block, q, sends, to):
        part = raw.at[
            pl.ds(pl.multiple_of(block * w, w), w),
            pl.ds(pl.multiple_of(q * chunk, chunk), chunk),
        ]
        return remote(part, part, sends.at[block, q], precv.at[block, q], {"col": to, "row": mr})

    loop(1, ncol, lambda t: diag_col(t, mc).start())

    def send_own(q):
        @pl.when(mc + 1 < ncol)
        def _():
            piece(mc, q, usend, mc + 1).start()

        @pl.when(mc > 0)
        def _():
            piece(mc, q, wsend, mc - 1).start()

    loop(0, CHUNKS, send_own)

    loop(1, ncol, lambda t: diag_col(t, lax.rem(mc + t, ncol)).wait_recv())
    loop(1, nrow, lambda t: diag_row(t, mr).start())
    loop(1, nrow, lambda t: rhs_copy(t, mr).start())

    def forward(e):
        s = e // CHUNKS + 1
        q = lax.rem(e, CHUNKS)

        @pl.when(jnp.logical_and(mc - s >= 0, mc + 1 < ncol))
        def _():
            piece(mc - s, q, usend, mc + 1).wait_recv()
            piece(mc - s, q, usend, mc + 1).start()

        @pl.when(jnp.logical_and(mc + s < ncol, mc > 0))
        def _():
            piece(mc + s, q, wsend, mc - 1).wait_recv()
            piece(mc + s, q, wsend, mc - 1).start()

    events = max(ncol - 2, 0) * CHUNKS
    early = events // 2
    each = -(-early // (nb // BS))

    ri = lax.broadcasted_iota(jnp.int32, (nb, nb), 0)
    ci = lax.broadcasted_iota(jnp.int32, (nb, nb), 1)
    aug[:, nb:] = jnp.where(ri == ci, 1.0, 0.0).astype(jnp.float32)
    loop(1, nrow, lambda t: diag_row(t, lax.rem(mr + t, nrow)).wait_recv())
    for r in range(nrow):
        parts = []
        for c in range(ncol):
            v = dslots[r, c]
            parts.append(
                jnp.concatenate([v[:, i * dc : (i + 1) * dc] for i in range(pack)], axis=0)
            )
        aug[r * dr : (r + 1) * dr, :nb] = jnp.concatenate(parts, axis=1)

    def block_step(b):
        loop(jnp.minimum(b * each, early), jnp.minimum((b + 1) * each, early), forward)
        here = pl.ds(pl.multiple_of(b * BS, BS), BS)
        panel = aug[here, :]
        rolled = pltpu.roll(panel[:, :nb], lax.rem(nb - b * BS, nb), 1)
        winv = eliminate(rolled[:, :BS])
        upper = dot(winv, panel)
        linv[here, :] = upper[:, nb:]

        @pl.when(b + 1 < nb // BS)
        def _():
            lane = lax.broadcasted_iota(jnp.int32, (BS, nb), 1)
            later = jnp.where(lane >= (b + 1) * BS, upper[:, :nb], 0.0)
            aug[...] = aug[...] - dot(later, upper, ((0,), (0,)))

    loop(0, nb // BS, block_step)
    loop(early, events, forward)

    loop(1, nrow, lambda t: rhs_copy(t, lax.rem(mr + t, nrow)).wait_recv())
    top = jnp.concatenate([rslots[r].T for r in range(nrow)], axis=0)
    rt = dot(linv[...], top).T
    lr_ref[slab_count:, :] = rt
    rs_ref[...] = pltpu.roll(rt, lax.rem(nb - mr * rk, nb), 1)[:, :rk]

    def finish(q):
        @pl.when(q == CHUNKS - 1)
        def _():
            @pl.when(root != mr)
            def _():
                left_copy(0).wait_recv()

        def arrived(t):
            block = lax.rem(mc + t, ncol)

            @pl.when(jnp.logical_or(
                jnp.logical_and(block < mc, mc + 1 >= ncol),
                jnp.logical_and(block > mc, mc <= 0),
            ))
            def _():
                piece(block, q, usend, mc).wait_recv()

        loop(1, ncol, arrived)

        @pl.when(jnp.logical_and(root == mr, slab_off // chunk == q))
        def _():
            left[...] = raw[:, pl.ds(slab_off, slab_count)]
            loop(1, nrow, lambda t: left_copy(t).start())

        @pl.when(q == CHUNKS - 1)
        def _():
            lr_ref[:slab_count, :] = dot(linv[...], left[...]).T

        at = pl.ds(pl.multiple_of(q * chunk, chunk), chunk)
        pt_ref[:, at] = dot(linv[...], raw[:, at])

    loop(0, CHUNKS, finish)

    loop(1, ncol, lambda t: diag_col(t, mc).wait_send())
    loop(1, nrow, lambda t: diag_row(t, mr).wait_send())
    loop(1, nrow, lambda t: rhs_copy(t, mr).wait_send())

    @pl.when(root == mr)
    def _():
        loop(1, nrow, lambda t: left_copy(t).wait_send())

    def sent(block):
        def chunk_sent(q):
            @pl.when(jnp.logical_and(block <= mc, mc + 1 < ncol))
            def _():
                piece(block, q, usend, mc + 1).wait_send()

            @pl.when(jnp.logical_and(block >= mc, mc > 0))
            def _():
                piece(block, q, wsend, mc - 1).wait_send()

        loop(0, CHUNKS, chunk_sent)

    loop(0, ncol, sent)


def update_kernel(w, slab_count, pt_ref, lr_ref, rs_ref, slab_ref, low_ref,
                  pf_ref, su_ref, rso_ref, ru_ref):
    mc = lax.axis_index("col")
    prod = dot(lr_ref[...], pt_ref[...])
    su_ref[...] = slab_ref[...] - prod[:slab_count]
    ru_ref[...] = low_ref[...] - prod[slab_count:]
    pf_ref[...] = pt_ref[pl.ds(pl.multiple_of(mc * w, w), w), :]
    rso_ref[...] = rs_ref[...]


def local(ncol, nrow, diag_block, panel_low, slab_rows, rhs_top, rhs_low):
    dr, dc = diag_block.shape
    rows, w = panel_low.shape
    nb = w * ncol
    slab_count = slab_rows.shape[0]
    nrhs, rk = rhs_top.shape
    pack = 128 // dc
    if dr % (8 * pack):
        pack = 1
    f32 = jnp.float32
    vm = pl.BlockSpec(memory_space=pltpu.VMEM)
    dma = pltpu.SemaphoreType.DMA
    pt, lr, rs = pl.pallas_call(
        functools.partial(gather_kernel, ncol, nrow, pack, slab_count),
        out_shape=(
            jax.ShapeDtypeStruct((nb, rows), f32),
            jax.ShapeDtypeStruct((slab_count + nrhs, nb), f32),
            jax.ShapeDtypeStruct((nrhs, rk), f32),
        ),
        in_specs=[pl.BlockSpec(memory_space=pl.ANY)] * 3,
        out_specs=(vm,) * 3,
        scratch_shapes=[
            pltpu.VMEM((dr, dc), f32),
            pltpu.VMEM((nrow, ncol, dr // pack, dc * pack), f32),
            pltpu.VMEM((nb, rows), f32),
            pltpu.VMEM((nb, slab_count), f32),
            pltpu.VMEM((nrow, nrhs, rk), f32),
            pltpu.VMEM((nb, 2 * nb), f32),
            pltpu.VMEM((nb, nb), f32),
            dma((3,)),
            dma((ncol,)), dma((ncol,)),
            dma((nrow,)), dma((nrow,)),
            dma((nrow,)), dma((nrow,)),
            dma((nrow,)), dma,
            dma((ncol, CHUNKS)), dma((ncol, CHUNKS)), dma((ncol, CHUNKS)),
        ],
        compiler_params=pltpu.CompilerParams(
            collective_id=0, has_side_effects=True, vmem_limit_bytes=40 * 1024 * 1024
        ),
    )(diag_block, panel_low.T, rhs_top)
    tile = rows // 4
    pf, su, rso, ru = pl.pallas_call(
        functools.partial(update_kernel, w, slab_count),
        grid=(4,),
        out_shape=(
            jax.ShapeDtypeStruct((w, rows), f32),
            jax.ShapeDtypeStruct(slab_rows.shape, f32),
            jax.ShapeDtypeStruct((nrhs, rk), f32),
            jax.ShapeDtypeStruct(rhs_low.shape, f32),
        ),
        in_specs=[
            pl.BlockSpec((nb, tile), lambda i: (0, i)),
            pl.BlockSpec((slab_count + nrhs, nb), lambda i: (0, 0)),
            pl.BlockSpec((nrhs, rk), lambda i: (0, 0)),
            pl.BlockSpec((slab_count, tile), lambda i: (0, i)),
            pl.BlockSpec((nrhs, tile), lambda i: (0, i)),
        ],
        out_specs=(
            pl.BlockSpec((w, tile), lambda i: (0, i)),
            pl.BlockSpec((slab_count, tile), lambda i: (0, i)),
            pl.BlockSpec((nrhs, rk), lambda i: (0, 0)),
            pl.BlockSpec((nrhs, tile), lambda i: (0, i)),
        ),
        compiler_params=pltpu.CompilerParams(vmem_limit_bytes=32 * 1024 * 1024),
    )(pt, lr, rs, slab_rows, rhs_low)
    return pf.T, su, rso, ru


def solution(mesh):
    ncol, nrow = mesh.shape["col"], mesh.shape["row"]
    return jax.shard_map(
        functools.partial(local, ncol, nrow),
        mesh=mesh,
        in_specs=(
            P("row", "col"),
            P(("groups", "row"), "col"),
            P("col", ("groups", "row")),
            P(("groups", "col"), "row"),
            P("col", ("groups", "row")),
        ),
        out_specs=(
            P(("groups", "row"), "col"),
            P("col", ("groups", "row")),
            P(("groups", "col"), "row"),
            P("col", ("groups", "row")),
        ),
        check_vma=False,
    )
```

time: 62.2 us -> 51.9 us (0.83)
  the two profiles are of different devices: /device:TPU:8 before, /device:TPU:0 now
where the time goes in v2:
time: 51.9 us; the launch traced here: 51.5 us
  Pallas kernels  46.1 us (89%)
  local copies, waits for them, and re-layouts  4.81 us (9%)
  between operations  0.66 us (1%)
    pallas_call x1, Pallas kernels, local(): pl.pallas_call(functools.partial(gather_kernel, ncol, nrow, pack, slab_co...  42.8 us
    unnamed x10, local copies, waits for them, and re-layouts  4.81 us
    pallas_call x1, Pallas kernels, local(): pl.pallas_call(functools.partial(update_kernel, w, slab_count), grid=(4,)...  3.27 us

profile of v2, /device:TPU:0, one launch (start us, length us, event | category | flops | bytes accessed | tf_op | source)
XLA Modules:
  0.0 51.5 jit_solution(7678430217480836038)
XLA Ops:
  0.6 0.0 copy-start.1
  0.6 1.0 %copy-done.1 = f32[2048,64]{0,1:T(8,128)S(1)} copy-done((f32[2048,64]{0,1:T(8,128)S(1)}, f32[2048,64]{0,1:T(8,128)}, u32[]{:S(2)}) %copy-start.1) | copy-done | bytes 524312
  1.7 0.0 copy-start.3
  1.7 0.8 %copy-done.3 = f32[64,64]{1,0:T(8,128)S(1)} copy-done((f32[64,64]{1,0:T(8,128)S(1)}, f32[64,64]{1,0:T(8,128)}, u32[]{:S(2)}) %copy-start.3) | copy-done | bytes 16408
  2.4 0.0 copy-start.4
  2.4 0.8 %copy-done.4 = f32[64,64]{1,0:T(8,128)S(1)} copy-done((f32[64,64]{1,0:T(8,128)S(1)}, f32[64,64]{1,0:T(8,128)}, u32[]{:S(2)}) %copy-start.4) | copy-done | bytes 16408
  3.2 42.8 %shard_map.84 = (f32[256,2048]{1,0:T(8,128)S(1)}, f32[192,256]{1,0:T(8,128)S(1)}, f32[64,64]{1,0:T(8,128)S(1)}) custom-call(f32[64,64]{1,0:T(8,128)S(1)} %copy-done.3, f32[64,2048]{1,0:T(8,128)S(1)} %bitcast.2, f32[64,64]{1,0:T(8,128)S(1)} %copy-done.4), custom_call_target="tpu_custom_call" | custom-call | tf_op jit(solution)/shard_map/pallas_call | solution.py:307
  46.0 0.0 copy-start
  46.0 1.2 %copy-done = f32[128,2048]{1,0:T(8,128)S(1)} copy-done((f32[128,2048]{1,0:T(8,128)S(1)}, f32[128,2048]{1,0:T(8,128)}, u32[]{:S(2)}) %copy-start) | copy-done | bytes 1048600
  47.2 0.0 copy-start.2
  47.2 1.0 %copy-done.2 = f32[64,2048]{1,0:T(8,128)S(1)} copy-done((f32[64,2048]{1,0:T(8,128)S(1)}, f32[64,2048]{1,0:T(8,128)}, u32[]{:S(2)}) %copy-start.2) | copy-done | bytes 524312
  48.2 3.3 %shard_map.85 = (f32[64,2048]{1,0:T(8,128)}, f32[128,2048]{1,0:T(8,128)}, f32[64,64]{1,0:T(8,128)}, f32[64,2048]{1,0:T(8,128)}) custom-call(f32[256,2048]{1,0:T(8,128)S(1)} %get-tuple-element.11.pt_ref, f32[192,256]{1,0:T(8,128)S(1)} %get-tuple-element.12.lr_ref, f32[64,64]{1,0:T(8,128)S(1)} %get-tuple-element.13.rs_ref, f32[128,2048]{1,0:T(8,128)S(1)} %copy-done, ...), custom_call_target="tpu_custom_call" | custom-call | tf_op jit(solution)/shard_map/pallas_call | solution.py:336
Async XLA Ops:
  0.6 1.0 %copy-start.1 = (f32[2048,64]{0,1:T(8,128)S(1)}, f32[2048,64]{0,1:T(8,128)}, u32[]{:S(2)}) copy-start(f32[2048,64]{0,1:T(8,128)} %param.6) | copy-start | bytes 1572868
  1.7 0.8 %copy-start.3 = (f32[64,64]{1,0:T(8,128)S(1)}, f32[64,64]{1,0:T(8,128)}, u32[]{:S(2)}) copy-start(f32[64,64]{1,0:T(8,128)} %diag_ref.1) | copy-start | bytes 49156
  2.4 0.8 %copy-start.4 = (f32[64,64]{1,0:T(8,128)S(1)}, f32[64,64]{1,0:T(8,128)}, u32[]{:S(2)}) copy-start(f32[64,64]{1,0:T(8,128)} %rhs_ref.1) | copy-start | bytes 49156
  46.0 1.2 %copy-start = (f32[128,2048]{1,0:T(8,128)S(1)}, f32[128,2048]{1,0:T(8,128)}, u32[]{:S(2)}) copy-start(f32[128,2048]{1,0:T(8,128)} %slab_ref.1) | copy-start | bytes 3145732
  47.2 1.0 %copy-start.2 = (f32[64,2048]{1,0:T(8,128)S(1)}, f32[64,2048]{1,0:T(8,128)}, u32[]{:S(2)}) copy-start(f32[64,2048]{1,0:T(8,128)} %low_ref.1) | copy-start | bytes 1572868

commit v3 on v2

--- a/solution.py
+++ b/solution.py
@@ -74,11 +74,12 @@
 
 def gather_kernel(
     ncol, nrow, pack, slab_count,
-    diag_ref, panel_ref, rhs_ref,
-    pt_ref, lr_ref, rs_ref,
-    dmine, dslots, raw, left, rslots, aug, linv,
+    diag_ref, panel_ref, rhs_ref, slab_ref, low_ref,
+    pf_out, su_out, rs_out, ru_out,
+    pf_ref, su_ref, rs_ref, ru_ref,
+    pt_ref, lr_ref, dmine, dslots, raw, left, rslots, aug, linv,
     local_sem, d1send, d1recv, d2send, d2recv, rsend, rrecv,
-    lsend, lrecv, usend, wsend, precv,
+    lsend, lrecv, usend, wsend, precv, osem,
 ):
     mc = lax.axis_index("col")
     mr = lax.axis_index("row")
@@ -117,6 +118,8 @@
         pltpu.make_async_copy(diag_ref, dmine, local_sem.at[0]),
         pltpu.make_async_copy(panel_ref, raw.at[mine, :], local_sem.at[1]),
         pltpu.make_async_copy(rhs_ref, rslots.at[mr], local_sem.at[2]),
+        pltpu.make_async_copy(slab_ref, su_ref, local_sem.at[3]),
+        pltpu.make_async_copy(low_ref, ru_ref, local_sem.at[4]),
     )
     for load in loads:
         load.start()
@@ -225,13 +228,35 @@
     rt = dot(linv[...], top).T
     lr_ref[slab_count:, :] = rt
     rs_ref[...] = pltpu.roll(rt, lax.rem(nb - mr * rk, nb), 1)[:, :rk]
+    rs_write = pltpu.make_async_copy(rs_ref, rs_out, local_sem.at[5])
+    rs_write.start()
+
+    loads[3].wait()
+    loads[4].wait()
+
+    def writes(q):
+        at = pl.ds(pl.multiple_of(q * chunk, chunk), chunk)
+        return [
+            pltpu.make_async_copy(here.at[:, at], there.at[:, at], osem.at[i, q])
+            for i, (here, there) in enumerate(
+                ((pf_ref, pf_out), (su_ref, su_out), (ru_ref, ru_out))
+            )
+        ]
+
+    def update(q):
+        at = pl.ds(pl.multiple_of(q * chunk, chunk), chunk)
+        prod = dot(lr_ref[...], pt_ref[:, at])
+        su_ref[:, at] = su_ref[:, at] - prod[:slab_count]
+        ru_ref[:, at] = ru_ref[:, at] - prod[slab_count:]
+        for write in writes(q):
+            write.start()
 
     def finish(q):
-        @pl.when(q == CHUNKS - 1)
-        def _():
-            @pl.when(root != mr)
-            def _():
-                left_copy(0).wait_recv()
+        @pl.when(jnp.logical_and(q == CHUNKS - 1, root != mr))
+        def _():
+            left_copy(0).wait_recv()
+            lr_ref[:slab_count, :] = dot(linv[...], left[...]).T
+            loop(0, CHUNKS - 1, update)
 
         def arrived(t):
             block = lax.rem(mc + t, ncol)
@@ -249,15 +274,28 @@
         def _():
             left[...] = raw[:, pl.ds(slab_off, slab_count)]
             loop(1, nrow, lambda t: left_copy(t).start())
-
-        @pl.when(q == CHUNKS - 1)
-        def _():
             lr_ref[:slab_count, :] = dot(linv[...], left[...]).T
+            loop(0, q, update)
 
         at = pl.ds(pl.multiple_of(q * chunk, chunk), chunk)
         pt_ref[:, at] = dot(linv[...], raw[:, at])
+        pf_ref[:, at] = pt_ref[mine, at]
+
+        @pl.when(jnp.logical_or(
+            jnp.logical_and(root == mr, q >= slab_off // chunk), q == CHUNKS - 1
+        ))
+        def _():
+            update(q)
 
     loop(0, CHUNKS, finish)
+
+    rs_write.wait()
+
+    def written(q):
+        for write in writes(q):
+            write.wait()
+
+    loop(0, CHUNKS, written)
 
     loop(1, ncol, lambda t: diag_col(t, mc).wait_send())
     loop(1, nrow, lambda t: diag_row(t, mr).wait_send())
@@ -282,14 +320,24 @@
     loop(0, ncol, sent)
 
 
-def update_kernel(w, slab_count, pt_ref, lr_ref, rs_ref, slab_ref, low_ref,
-                  pf_ref, su_ref, rso_ref, ru_ref):
-    mc = lax.axis_index("col")
-    prod = dot(lr_ref[...], pt_ref[...])
-    su_ref[...] = slab_ref[...] - prod[:slab_count]
-    ru_ref[...] = low_ref[...] - prod[slab_count:]
-    pf_ref[...] = pt_ref[pl.ds(pl.multiple_of(mc * w, w), w), :]
-    rso_ref[...] = rs_ref[...]
+def write_kernel(count, *refs):
+    ins, outs, held = refs[:count], refs[count : 2 * count], refs[2 * count : 3 * count]
+    load_sem, store_sem = refs[3 * count :]
+    loads, stores = [], []
+    for src, dst, buf in zip(ins, outs, held):
+        size = 32 if src.shape[0] % 32 == 0 else src.shape[0]
+        for first in range(0, src.shape[0], size):
+            at = pl.ds(first, size)
+            i = len(loads)
+            loads.append(pltpu.make_async_copy(src.at[at, :], buf.at[at, :], load_sem.at[i]))
+            stores.append(pltpu.make_async_copy(buf.at[at, :], dst.at[at, :], store_sem.at[i]))
+    for load in loads:
+        load.start()
+    for load, store in zip(loads, stores):
+        load.wait()
+        store.start()
+    for store in stores:
+        store.wait()
 
 
 def local(ncol, nrow, diag_block, panel_low, slab_rows, rhs_top, rhs_low):
@@ -302,18 +350,23 @@
     if dr % (8 * pack):
         pack = 1
     f32 = jnp.float32
-    vm = pl.BlockSpec(memory_space=pltpu.VMEM)
+    hbm = pl.BlockSpec(memory_space=pltpu.HBM)
     dma = pltpu.SemaphoreType.DMA
-    pt, lr, rs = pl.pallas_call(
+    outs = (
+        jax.ShapeDtypeStruct((w, rows), f32),
+        jax.ShapeDtypeStruct(slab_rows.shape, f32),
+        jax.ShapeDtypeStruct((nrhs, rk), f32),
+        jax.ShapeDtypeStruct(rhs_low.shape, f32),
+    )
+    done = pl.pallas_call(
         functools.partial(gather_kernel, ncol, nrow, pack, slab_count),
-        out_shape=(
-            jax.ShapeDtypeStruct((nb, rows), f32),
-            jax.ShapeDtypeStruct((slab_count + nrhs, nb), f32),
-            jax.ShapeDtypeStruct((nrhs, rk), f32),
-        ),
-        in_specs=[pl.BlockSpec(memory_space=pl.ANY)] * 3,
-        out_specs=(vm,) * 3,
+        out_shape=outs,
+        in_specs=[hbm] * 5,
+        out_specs=(hbm,) * 4,
         scratch_shapes=[
+            *(pltpu.VMEM(out.shape, f32) for out in outs),
+            pltpu.VMEM((nb, rows), f32),
+            pltpu.VMEM((slab_count + nrhs, nb), f32),
             pltpu.VMEM((dr, dc), f32),
             pltpu.VMEM((nrow, ncol, dr // pack, dc * pack), f32),
             pltpu.VMEM((nb, rows), f32),
@@ -321,43 +374,31 @@
             pltpu.VMEM((nrow, nrhs, rk), f32),
             pltpu.VMEM((nb, 2 * nb), f32),
             pltpu.VMEM((nb, nb), f32),
-            dma((3,)),
+            dma((6,)),
             dma((ncol,)), dma((ncol,)),
             dma((nrow,)), dma((nrow,)),
             dma((nrow,)), dma((nrow,)),
             dma((nrow,)), dma,
             dma((ncol, CHUNKS)), dma((ncol, CHUNKS)), dma((ncol, CHUNKS)),
+            dma((3, CHUNKS)),
         ],
         compiler_params=pltpu.CompilerParams(
-            collective_id=0, has_side_effects=True, vmem_limit_bytes=40 * 1024 * 1024
+            collective_id=0, has_side_effects=True, vmem_limit_bytes=61 * 1024 * 1024
         ),
-    )(diag_block, panel_low.T, rhs_top)
-    tile = rows // 4
-    pf, su, rso, ru = pl.pallas_call(
-        functools.partial(update_kernel, w, slab_count),
-        grid=(4,),
-        out_shape=(
-            jax.ShapeDtypeStruct((w, rows), f32),
-            jax.ShapeDtypeStruct(slab_rows.shape, f32),
-            jax.ShapeDtypeStruct((nrhs, rk), f32),
-            jax.ShapeDtypeStruct(rhs_low.shape, f32),
-        ),
-        in_specs=[
-            pl.BlockSpec((nb, tile), lambda i: (0, i)),
-            pl.BlockSpec((slab_count + nrhs, nb), lambda i: (0, 0)),
-            pl.BlockSpec((nrhs, rk), lambda i: (0, 0)),
-            pl.BlockSpec((slab_count, tile), lambda i: (0, i)),
-            pl.BlockSpec((nrhs, tile), lambda i: (0, i)),
+    )(diag_block, panel_low.T, rhs_top, slab_rows, rhs_low)
+    pieces = sum(-(-out.shape[0] // 32) for out in outs)
+    pf, su, rs, ru = pl.pallas_call(
+        functools.partial(write_kernel, len(outs)),
+        out_shape=outs,
+        in_specs=[hbm] * 4,
+        out_specs=(hbm,) * 4,
+        scratch_shapes=[
+            *(pltpu.VMEM(out.shape, f32) for out in outs),
+            dma((pieces,)), dma((pieces,)),
         ],
-        out_specs=(
-            pl.BlockSpec((w, tile), lambda i: (0, i)),
-            pl.BlockSpec((slab_count, tile), lambda i: (0, i)),
-            pl.BlockSpec((nrhs, rk), lambda i: (0, 0)),
-            pl.BlockSpec((nrhs, tile), lambda i: (0, i)),
-        ),
-        compiler_params=pltpu.CompilerParams(vmem_limit_bytes=32 * 1024 * 1024),
-    )(pt, lr, rs, slab_rows, rhs_low)
-    return pf.T, su, rso, ru
+        compiler_params=pltpu.CompilerParams(vmem_limit_bytes=61 * 1024 * 1024),
+    )(*done)
+    return pf.T, su, rs, ru
 
 
 def solution(mesh):

time: 51.9 us -> 47 us (0.906)
  local copies, waits for them, and re-layouts: 4.81 us -> 0 us
    unnamed x10 -> x0, local copies, waits for them, and re-layouts: 4.81 us -> none
    pallas_call x1, Pallas kernels: 42.8 us -> 43.8 us  [local(): pl.pallas_call(functools.partial(gather_kernel, ncol, nrow, pack, slab_co...]
    pallas_call x1, Pallas kernels: 3.27 us -> 2.44 us  [local(): pl.pallas_call(functools.partial(write_kernel, len(outs)), out_shape=outs...]
where the time goes in v3:
time: 47 us; the launch traced here: 46.9 us
  Pallas kernels  46.2 us (98%)
  between operations  0.64 us (1%)
    pallas_call x1, Pallas kernels, local(): pl.pallas_call(functools.partial(gather_kernel, ncol, nrow, pack, slab_co...  43.8 us
    pallas_call x1, Pallas kernels, local(): pl.pallas_call(functools.partial(write_kernel, len(outs)), out_shape=outs...  2.44 us

profile of v3, /device:TPU:0, one launch (start us, length us, event | category | flops | bytes accessed | tf_op | source)
XLA Modules:
  0.0 46.9 jit_solution(45436274638258107)
XLA Ops:
  0.6 43.8 %shard_map.84 = (f32[64,2048]{1,0:T(8,128)}, f32[128,2048]{1,0:T(8,128)}, f32[64,64]{1,0:T(8,128)}, f32[64,2048]{1,0:T(8,128)}) custom-call(f32[64,64]{1,0:T(8,128)} %diag_ref.1, f32[64,2048]{1,0:T(8,128)} %bitcast.2, f32[64,64]{1,0:T(8,128)} %rhs_ref.1, f32[128,2048]{1,0:T(8,128)} %slab_ref.1, f32[64,2048]{1,0:T(8,128)} %low_ref.1), custom_call_target="tpu_custom_call" | custom-call | tf_op jit(solution)/shard_map/pallas_call | solution.py:361
  44.4 2.4 %shard_map.85 = (f32[64,2048]{1,0:T(8,128)}, f32[128,2048]{1,0:T(8,128)}, f32[64,64]{1,0:T(8,128)}, f32[64,2048]{1,0:T(8,128)}) custom-call(f32[64,2048]{1,0:T(8,128)} %get-tuple-element.12.refs_0_, f32[128,2048]{1,0:T(8,128)} %get-tuple-element.13.refs_1_, f32[64,64]{1,0:T(8,128)} %get-tuple-element.14.refs_2_, f32[64,2048]{1,0:T(8,128)} %get-tuple-element.15.refs_3_), custom_call_target="tpu_custom_call" | custom-call | tf_op jit(solution)/shard_map/pallas_call | solution.py:390

commit v4 on v3

--- a/solution.py
+++ b/solution.py
@@ -9,7 +9,7 @@
 
 MESH = pl.DeviceIdType.MESH
 BS = 64
-CHUNKS = 4
+CHUNKS = 8
 PIVOTS = 8
 HIGH = lax.Precision.HIGHEST
 

time: 47 us -> 48.3 us (1.028)
  the two profiles are of different devices: /device:TPU:0 before, /device:TPU:2 now
where the time goes in v4:
time: 48.3 us; the launch traced here: 48.1 us
  Pallas kernels  47.5 us (98%)
  between operations  0.64 us (1%)
    pallas_call x1, Pallas kernels, local(): pl.pallas_call(functools.partial(gather_kernel, ncol, nrow, pack, slab_co...  45.1 us
    pallas_call x1, Pallas kernels, local(): pl.pallas_call(functools.partial(write_kernel, len(outs)), out_shape=outs...  2.44 us

profile of v4, /device:TPU:2, one launch (start us, length us, event | category | flops | bytes accessed | tf_op | source)
XLA Modules:
  0.0 48.1 jit_solution(13091892543295443547)
XLA Ops:
  0.6 45.1 %shard_map.84 = (f32[64,2048]{1,0:T(8,128)}, f32[128,2048]{1,0:T(8,128)}, f32[64,64]{1,0:T(8,128)}, f32[64,2048]{1,0:T(8,128)}) custom-call(f32[64,64]{1,0:T(8,128)} %diag_ref.1, f32[64,2048]{1,0:T(8,128)} %bitcast.2, f32[64,64]{1,0:T(8,128)} %rhs_ref.1, f32[128,2048]{1,0:T(8,128)} %slab_ref.1, f32[64,2048]{1,0:T(8,128)} %low_ref.1), custom_call_target="tpu_custom_call" | custom-call | tf_op jit(solution)/shard_map/pallas_call | solution.py:361
  45.7 2.4 %shard_map.85 = (f32[64,2048]{1,0:T(8,128)}, f32[128,2048]{1,0:T(8,128)}, f32[64,64]{1,0:T(8,128)}, f32[64,2048]{1,0:T(8,128)}) custom-call(f32[64,2048]{1,0:T(8,128)} %get-tuple-element.12.refs_0_, f32[128,2048]{1,0:T(8,128)} %get-tuple-element.13.refs_1_, f32[64,64]{1,0:T(8,128)} %get-tuple-element.14.refs_2_, f32[64,2048]{1,0:T(8,128)} %get-tuple-element.15.refs_3_), custom_call_target="tpu_custom_call" | custom-call | tf_op jit(solution)/shard_map/pallas_call | solution.py:390
